TPU v7x, 32 devices: a whole 2x2x4 slice. The times are simulated.
32 devices in a mesh: groups: 2 (over x), tm: 16 (over z, y, core).
Axes of the slice: x: 2, y: 2, z: 4, core: 2. Of those that a mesh axis runs over, the one named last changes fastest.
Arguments:
- sharded_latents: bfloat16 [32, 6144], P('groups', 'tm'), parts along dimension 0, may hold values from -6 to 6
- sample_frame_count: int32 [16], P('groups'), parts along dimension 0, may hold values from 5 to 8, as said below
- entry_kernel: bfloat16 [27, 16, 384], replicated, may hold values from -0.3125 to 0.3125
- entry_bias: float32 [384], replicated, may hold values from -3 to 3
- norm_scale_gain: float32 [384], replicated, may hold values from 0.25 to 1.75
- residual_kernel: bfloat16 [27, 384, 384], P(None, 'tm'), may hold values from -0.0625 to 0.0625
- residual_bias: float32 [384], replicated, may hold values from -3 to 3
Outputs:
- decoded: bfloat16 [128, 6, 16, 384], P(('groups', 'tm')), parts along dimension 0
There are 2 independent parts, one for each index of `groups`. A program takes and returns all parts, laid end to end along the dimension named above; an argument that names none is the same for every part. Nothing has to cross between parts.
Inputs may be any that keep to these rules, and one draw needn't show every extreme that they name: `sample_frame_count`: every sample has more than half of its 8 frames valid; some sample has all of them valid.
All inputs are finite; a program needn't handle non-finite values.
Results may differ from a plain program's by a relative error of at most 0.009.
Values may be sent and summed in bfloat16 or wider, within the bound.
A program may use at most 64 MiB of HBM per device.

v0:
```python
import jax
import jax.numpy as jnp
from jax import lax
from jax.sharding import PartitionSpec as P

LATENT_CHANNELS = 16
C = 384
PROMPT_SAMPLES = 8
BLOCK_FRAMES = 4
LATENT_ROWS = 6
LATENT_COLUMNS = 16


def from_behind(block, axis, distance):
    devices = range(lax.axis_size(axis))
    route = [(i - distance, i) for i in devices if i - distance in devices]
    return lax.ppermute(block, axis, route)


def causal_conv(frames, weight):
    frames_out = frames.shape[0] - 2
    inputs = frames.shape[3]
    padded = jnp.pad(frames, ((0, 0), (1, 1), (1, 1), (0, 0)))
    total = jnp.zeros((frames_out * LATENT_ROWS * LATENT_COLUMNS, weight.shape[2]), jnp.float32)
    for time_tap in range(3):
        for row_tap in range(3):
            for col_tap in range(3):
                window = padded[
                    time_tap : time_tap + frames_out,
                    row_tap : row_tap + LATENT_ROWS,
                    col_tap : col_tap + LATENT_COLUMNS,
                    :,
                ]
                window = window.reshape(frames_out * LATENT_ROWS * LATENT_COLUMNS, inputs)
                tap = 9 * time_tap + 3 * row_tap + col_tap
                total = total + jnp.dot(window, weight[tap], preferred_element_type=jnp.float32)
    return total


def activate(stream, norm_scale_gain):
    values = stream.astype(jnp.float32)
    scale = lax.rsqrt(jnp.mean(values * values, axis=-1, keepdims=True) + 1e-06)
    return jax.nn.silu(values * scale * norm_scale_gain).astype(jnp.bfloat16)


def to_cells(planes):
    return jnp.transpose(
        planes.reshape(planes.shape[0], LATENT_CHANNELS, LATENT_ROWS, LATENT_COLUMNS), (0, 2, 3, 1)
    )


def shards(
    sharded_latents,
    sample_frame_count,
    entry_kernel,
    entry_bias,
    norm_scale_gain,
    residual_kernel,
    residual_bias,
):
    gathered_latents = lax.all_to_all(
        sharded_latents, "tm", split_axis=0, concat_axis=1, tiled=True
    )
    latent_volume = gathered_latents.reshape(
        BLOCK_FRAMES, LATENT_CHANNELS, LATENT_ROWS * LATENT_COLUMNS
    )
    position = lax.axis_index("tm")
    block = position // PROMPT_SAMPLES
    sample = position % PROMPT_SAMPLES
    keep = block > 0
    earlier = from_behind(latent_volume, "tm", PROMPT_SAMPLES)
    earlier = jnp.where(keep, earlier, jnp.zeros_like(earlier))
    frames = to_cells(jnp.concatenate([earlier, latent_volume], axis=0))
    widened = (causal_conv(frames, entry_kernel) + entry_bias).astype(jnp.bfloat16)
    active_all = activate(widened, norm_scale_gain).reshape(
        BLOCK_FRAMES + 2, LATENT_ROWS, LATENT_COLUMNS, C
    )
    behind = jnp.where(keep, active_all[:2], jnp.zeros_like(active_all[:2]))
    extended = jnp.concatenate([behind, active_all[2:]], axis=0)
    stream = widened[2 * LATENT_ROWS * LATENT_COLUMNS :]
    kernel_all = lax.all_gather(residual_kernel, "tm", axis=1, tiled=True)
    branch = causal_conv(extended, kernel_all)
    total = (stream.astype(jnp.float32) + (branch + residual_bias)).reshape(
        BLOCK_FRAMES, LATENT_ROWS, LATENT_COLUMNS, C
    )
    limit = jnp.sum(jnp.where(jnp.arange(PROMPT_SAMPLES) == sample, sample_frame_count, 0))
    frame_index = block * BLOCK_FRAMES + jnp.arange(BLOCK_FRAMES)
    valid = (frame_index < limit)[:, None, None, None]
    return jnp.where(valid, total, jnp.zeros_like(total)).astype(jnp.bfloat16)


def solution(mesh):
    in_specs = (P("groups", "tm"), P("groups"), P(), P(), P(), P(None, "tm", None), P())
    out_specs = P(("groups", "tm"), None, None, None)
    return jax.shard_map(shards, mesh=mesh, in_specs=in_specs, out_specs=out_specs, check_vma=False)
```

profile of v0, /device:TPU:0, one launch (start us, length us, event | category | flops | bytes accessed | tf_op | source)
XLA Modules:
  0.0 109.1 jit_solution(9590959347050248216)
XLA Ops:
  6.5 0.7 all-gather.2.cloned.1.call-update
  7.3 0.5 broadcast.36
  7.8 1.4 %reduce.2 = bf16[16,384]{1,0:T(8,128)(2,1)S(1)} reduce(bf16[16,1,384]{2,0,1:T(8,128)(2,1)} %bitcast.334, bf16[]{:T(256)} %broadcast.36), dimensions={1}, to_apply=%copy.62.reduce_sub_computation | reduce | bytes 24578 | tf_op jit(solution)/shard_map/all_to_all | solution.py:61
  9.1 0.7 reshape.257
  9.8 7.4 %all-to-all-start = ((bf16[16,2,192]{2,1,0:T(2,128)(2,1)}), bf16[16,2,192]{2,1,0:T(2,128)(2,1)S(1)}, u32[]{:S(2)}, u32[]{:S(2)}) async-start(bf16[16,2,192]{2,1,0:T(2,128)(2,1)} %reshape.257), calls=%async_computation | async-start | bytes 32768 | tf_op jit(solution)/shard_map/all_to_all | solution.py:61
  17.2 1.3 %fusion.70 = s32[]{:T(128)} fusion(s32[8]{0:T(128)} %param.8, s32[]{:T(128)S(6)} %select_n.39), kind=kLoop, calls=%fused_computation.186 | loop fusion | flops 23 | bytes 40 | tf_op jit(solution)/shard_map/reduce_sum | solution.py:86
  18.5 5.2 %all-to-all-done = bf16[16,2,192]{2,1,0:T(2,128)(2,1)S(1)} async-done(((bf16[16,2,192]{2,1,0:T(2,128)(2,1)}), bf16[16,2,192]{2,1,0:T(2,128)(2,1)S(1)}, u32[]{:S(2)}, u32[]{:S(2)}) %all-to-all-start) | async-done | bytes 12320 | tf_op jit(solution)/shard_map/all_to_all | solution.py:61
  24.0 2.4 %collective-permute-start = (bf16[4,16,96]{2,1,0:T(8,128)(2,1)S(1)}, bf16[4,16,96]{2,1,0:T(8,128)(2,1)S(1)}, u32[]{:S(2)}, u32[]{:S(2)}) collective-permute-start(bf16[4,16,96]{2,1,0:T(8,128)(2,1)S(1)} %reshape.200), channel_id=1, source_target_pairs={{0,8},{1,9},{2,10},{3,11},{4,12},{5,13},{6,14},{7,15},{16,24},{17,... | collective-permute-start | bytes 36872 | tf_op jit(solution)/shard_map/ppermute | solution.py:17
  26.4 0.6 add_compare_fusion
  27.2 0.7 collective-permute-done
  28.1 0.4 pad_slice_fusion.30
  28.5 0.8 reshape.201
  29.3 0.6 pad_slice_fusion.28
  29.9 0.8 reshape.202
  30.7 0.8 reshape.203
  31.6 0.8 reshape.204
  32.4 0.8 reshape.205
  33.2 0.8 reshape.206
  34.0 0.8 reshape.207
  34.8 0.8 reshape.208
  35.7 0.8 reshape.209
  36.5 0.8 reshape.210
  37.3 0.5 pad_slice_fusion.29
  37.9 0.8 reshape.211
  38.7 0.8 reshape.212
  42.8 1.0 fusion.41
  43.8 1.0 convolution_add_fusion.25
  44.9 1.1 convolution_add_fusion.24
  47.6 0.3 convolution_add_fusion.18
  52.1 0.5 convolution_add_fusion.4
  53.6 0.4 fusion.4
  54.0 0.3 fusion.11
  54.5 0.9 fusion.13
  55.4 1.2 %pad_slice_fusion.1 = (bf16[4,6,16,384]{3,2,1,0:T(8,128)(2,1)}, bf16[4,6,16,384]{3,2,1,0:T(8,128)(2,1)}, bf16[4,6,16,384]{3,2,1,0:T(8,128)(2,1)}, bf16[4,6,16,384]{3,2,1,0:T(8,128)(2,1)}, bf16[4,6,16,384]{3,2,1,0:T(8,128)(2,1)}) fusion(bf16[6,6,16,384]{3,2,1,0:T(8,128)(2,1)S(1)} %pad_maximum_fusion), kind=kLoop, calls=%fused_computation.1 | loop fusion | bytes 1916928 | tf_op jit(solution)/shard_map/slice | solution.py:28
  56.6 2.2 %pad_slice_fusion = (bf16[4,6,16,384]{3,2,1,0:T(8,128)(2,1)}, bf16[4,6,16,384]{3,2,1,0:T(8,128)(2,1)}, bf16[4,6,16,384]{3,2,1,0:T(8,128)(2,1)}, bf16[4,6,16,384]...) fusion(bf16[6,6,16,384]{3,2,1,0:T(8,128)(2,1)S(1)} %pad_maximum, ...), kind=kLoop, calls=%fused_computation | loop fusion | bytes 6045696 | tf_op jit(solution)/shard_map/slice | solution.py:28
  58.8 26.1 %all-gather.2.cloned.1.call-done = bf16[27,384,384]{2,1,0:T(8,128)(2,1)} async-done(((bf16[27,24,384]{2,1,0:T(8,128)(2,1)}), bf16[27,384,384]{2,1,0:T(8,128)(2,1)}) %all-gather.2.cloned.1.call-update) | async-done | bytes 7962640 | tf_op jit(solution)/shard_map/all_gather | solution.py:81
  84.9 1.5 %fusion.14 = f32[384,384]{1,0:T(8,128)S(1)} fusion(bf16[384,384]{1,0:T(8,128)(2,1)} %bitcast.333, bf16[27,384,384]{2,1,0:T(8,128)(2,1)} %all-gather.2.cloned.1.call-done), kind=kOutput, calls=%fused_computation.125 | convolution fusion | flops 113246208 | bytes 1179648 | tf_op jit(solution)/shard_map/dot_general | solution.py:36
  86.5 2.0 %convolution_add_fusion.51 = f32[384,384]{1,0:T(8,128)S(1)} fusion(f32[384,384]{1,0:T(8,128)S(1)} %fusion.14, bf16[384,384]{1,0:T(8,128)(2,1)} %bitcast.324, bf16[27,384,384]{2,1,0:T(8,128)(2,1)} %all-gather.2.cloned.1.call-done), kind=kOutput, calls=%fused_computation.79 | convolution fusion | flops 113393664 | bytes 1769472 | tf_op jit(solution)/shard_map/dot_general | solution.py:36
  88.5 1.4 %convolution_add_fusion.50 = f32[384,384]{1,0:T(8,128)S(1)} fusion(f32[384,384]{1,0:T(8,128)S(1)} %convolution_add_fusion.51, bf16[384,384]{1,0:T(8,128)(2,1)} %bitcast.323, bf16[27,384,384]{2,1,0:T(8,128)(2,1)} %all-gather.2.cloned.1.call-done), kind=kOutput, calls=%fused_computation.78 | convolution fusion | flops 113393664 | bytes 1769472 | tf_op jit(solution)/shard_map/dot_general | solution.py:36
  89.9 1.4 %convolution_add_fusion.49 = f32[384,384]{1,0:T(8,128)S(1)} fusion(f32[384,384]{1,0:T(8,128)S(1)} %convolution_add_fusion.50, bf16[384,384]{1,0:T(8,128)(2,1)} %bitcast.322, bf16[27,384,384]{2,1,0:T(8,128)(2,1)} %all-gather.2.cloned.1.call-done), kind=kOutput, calls=%fused_computation.77 | convolution fusion | flops 113393664 | bytes 1769472 | tf_op jit(solution)/shard_map/dot_general | solution.py:36
  91.3 1.4 %convolution_add_fusion.48 = f32[384,384]{1,0:T(8,128)S(1)} fusion(f32[384,384]{1,0:T(8,128)S(1)} %convolution_add_fusion.49, bf16[384,384]{1,0:T(8,128)(2,1)} %bitcast.327, bf16[27,384,384]{2,1,0:T(8,128)(2,1)} %all-gather.2.cloned.1.call-done), kind=kOutput, calls=%fused_computation.76 | convolution fusion | flops 113393664 | bytes 1769472 | tf_op jit(solution)/shard_map/dot_general | solution.py:36
  92.7 1.3 %convolution_add_fusion.47 = f32[384,384]{1,0:T(8,128)S(1)} fusion(f32[384,384]{1,0:T(8,128)S(1)} %convolution_add_fusion.48, bf16[384,384]{1,0:T(8,128)(2,1)} %bitcast.321, bf16[27,384,384]{2,1,0:T(8,128)(2,1)S(1)} %copy-done), kind=kOutput, calls=%fused_computation.75 | convolution fusion | flops 113393664 | bytes 1769472 | tf_op jit(solution)/shard_map/dot_general | solution.py:36
  94.0 0.3 convolution_add_fusion.46
  94.4 0.3 convolution_add_fusion.45
  94.7 0.3 convolution_add_fusion.44
  95.1 0.3 convolution_add_fusion.43
  95.4 0.3 convolution_add_fusion.42
  95.8 0.3 convolution_add_fusion.41
  96.1 0.3 convolution_add_fusion.40
  96.5 0.3 convolution_add_fusion.39
  96.8 0.3 convolution_add_fusion.38
  97.2 0.3 convolution_add_fusion.37
  97.5 0.3 convolution_add_fusion.36
  97.9 0.3 convolution_add_fusion.35
  98.2 0.3 convolution_add_fusion.34
  98.6 0.3 convolution_add_fusion.33
  98.9 0.3 convolution_add_fusion.32
  99.3 0.3 convolution_add_fusion.31
  99.6 0.3 convolution_add_fusion.30
  100.0 0.3 convolution_add_fusion.29
  100.3 0.3 convolution_add_fusion.28
  100.7 0.3 convolution_add_fusion.27
  101.0 0.4 fusion.3
  101.4 0.8 select_convert_fusion
  (125 shorter events, 10.9 us)
Async XLA Ops:
  6.5 78.4 %all-gather.2.cloned.1.call-start = ((), (), s32[]{:S(2)}) async-start(), calls=%async_computation.1 | async-start | bytes 8460288 | tf_op jit(solution)/shard_map/all_gather | solution.py:81
  9.8 13.9 %all-to-all-start = ((bf16[16,2,192]{2,1,0:T(2,128)(2,1)}), bf16[16,2,192]{2,1,0:T(2,128)(2,1)S(1)}, u32[]{:S(2)}, u32[]{:S(2)}) async-start(bf16[16,2,192]{2,1,0:T(2,128)(2,1)} %reshape.257), calls=%async_computation | async-start | bytes 32768 | tf_op jit(solution)/shard_map/all_to_all | solution.py:61
  24.0 3.9 %collective-permute-start = (bf16[4,16,96]{2,1,0:T(8,128)(2,1)S(1)}, bf16[4,16,96]{2,1,0:T(8,128)(2,1)S(1)}, u32[]{:S(2)}, u32[]{:S(2)}) collective-permute-start(bf16[4,16,96]{2,1,0:T(8,128)(2,1)S(1)} %reshape.200), channel_id=1, source_target_pairs={{0,8},{1,9},{2,10},{3,11},{4,12},{5,13},{6,14},{7,15},{16,24},{17,... | collective-permute-start | bytes 36872 | tf_op jit(solution)/shard_map/ppermute | solution.py:17
  37.8 8.2 %copy-start.13 = (bf16[576,16]{0,1:T(8,128)(2,1)S(1)}, bf16[576,16]{0,1:T(8,128)(2,1)}, u32[]{:S(2)}) copy-start(bf16[576,16]{0,1:T(8,128)(2,1)} %reshape.204) | copy-start | bytes 55300
  38.6 7.7 %copy-start.14 = (bf16[576,16]{0,1:T(8,128)(2,1)S(1)}, bf16[576,16]{0,1:T(8,128)(2,1)}, u32[]{:S(2)}) copy-start(bf16[576,16]{0,1:T(8,128)(2,1)} %reshape.205) | copy-start | bytes 55300
  38.7 4.1 %copy-start.12 = (bf16[27,16,384]{2,1,0:T(8,128)(2,1)S(1)}, bf16[27,16,384]{2,1,0:T(8,128)(2,1)}, u32[]{:S(2)}) copy-start(bf16[27,16,384]{2,1,0:T(8,128)(2,1)} %param.9) | copy-start | bytes 995332
  39.9 6.7 %copy-start.15 = (bf16[576,16]{0,1:T(8,128)(2,1)S(1)}, bf16[576,16]{0,1:T(8,128)(2,1)}, u32[]{:S(2)}) copy-start(bf16[576,16]{0,1:T(8,128)(2,1)} %reshape.206) | copy-start | bytes 55300
  40.6 6.4 %copy-start.16 = (bf16[576,16]{0,1:T(8,128)(2,1)S(1)}, bf16[576,16]{0,1:T(8,128)(2,1)}, u32[]{:S(2)}) copy-start(bf16[576,16]{0,1:T(8,128)(2,1)} %reshape.207) | copy-start | bytes 55300
  41.2 6.1 %copy-start.17 = (bf16[576,16]{0,1:T(8,128)(2,1)S(1)}, bf16[576,16]{0,1:T(8,128)(2,1)}, u32[]{:S(2)}) copy-start(bf16[576,16]{0,1:T(8,128)(2,1)} %reshape.208) | copy-start | bytes 55300
  41.9 5.7 %copy-start.18 = (bf16[576,16]{0,1:T(8,128)(2,1)S(1)}, bf16[576,16]{0,1:T(8,128)(2,1)}, u32[]{:S(2)}) copy-start(bf16[576,16]{0,1:T(8,128)(2,1)} %reshape.209) | copy-start | bytes 55300
  42.5 5.4 %copy-start.19 = (bf16[576,16]{0,1:T(8,128)(2,1)S(1)}, bf16[576,16]{0,1:T(8,128)(2,1)}, u32[]{:S(2)}) copy-start(bf16[576,16]{0,1:T(8,128)(2,1)} %reshape.210) | copy-start | bytes 55300
  43.8 4.4 %copy-start.20 = (bf16[576,16]{0,1:T(8,128)(2,1)S(1)}, bf16[576,16]{0,1:T(8,128)(2,1)}, u32[]{:S(2)}) copy-start(bf16[576,16]{0,1:T(8,128)(2,1)} %reshape.211) | copy-start | bytes 55300
  44.9 3.7 %copy-start.21 = (bf16[576,16]{0,1:T(8,128)(2,1)S(1)}, bf16[576,16]{0,1:T(8,128)(2,1)}, u32[]{:S(2)}) copy-start(bf16[576,16]{0,1:T(8,128)(2,1)} %reshape.212) | copy-start | bytes 55300
  50.5 3.1 %copy-start.22 = (f32[384]{0:T(512)S(1)}, f32[384]{0:T(512)}, u32[]{:S(2)}) copy-start(f32[384]{0:T(512)} %param.10) | copy-start | bytes 4612
  50.8 3.2 %copy-start.23 = (f32[384]{0:T(512)S(1)}, f32[384]{0:T(512)}, u32[]{:S(2)}) copy-start(f32[384]{0:T(512)} %param.11) | copy-start | bytes 4612
  84.9 7.8 %copy-start = (bf16[27,384,384]{2,1,0:T(8,128)(2,1)S(1)}, bf16[27,384,384]{2,1,0:T(8,128)(2,1)}, u32[]{:S(2)}) copy-start(bf16[27,384,384]{2,1,0:T(8,128)(2,1)} %all-gather.2.cloned.1.call-done) | copy-start | bytes 23887876
  84.9 9.1 %copy-start.5 = (bf16[4,6,16,384]{3,2,1,0:T(8,128)(2,1)S(1)}, bf16[4,6,16,384]{3,2,1,0:T(8,128)(2,1)}, u32[]{:S(2)}) copy-start(bf16[4,6,16,384]{3,2,1,0:T(8,128)(2,1)} %get-tuple-element.10) | copy-start | bytes 884740
  84.9 9.5 %copy-start.4 = (bf16[4,6,16,384]{3,2,1,0:T(8,128)(2,1)S(1)}, bf16[4,6,16,384]{3,2,1,0:T(8,128)(2,1)}, u32[]{:S(2)}) copy-start(bf16[4,6,16,384]{3,2,1,0:T(8,128)(2,1)} %get-tuple-element.11) | copy-start | bytes 884740
  84.9 9.8 %copy-start.3 = (bf16[4,6,16,384]{3,2,1,0:T(8,128)(2,1)S(1)}, bf16[4,6,16,384]{3,2,1,0:T(8,128)(2,1)}, u32[]{:S(2)}) copy-start(bf16[4,6,16,384]{3,2,1,0:T(8,128)(2,1)} %get-tuple-element.12) | copy-start | bytes 884740
  84.9 10.2 %copy-start.2 = (bf16[4,6,16,384]{3,2,1,0:T(8,128)(2,1)S(1)}, bf16[4,6,16,384]{3,2,1,0:T(8,128)(2,1)}, u32[]{:S(2)}) copy-start(bf16[4,6,16,384]{3,2,1,0:T(8,128)(2,1)} %get-tuple-element.13) | copy-start | bytes 884740
  86.4 9.0 %copy-start.1 = (bf16[4,6,16,384]{3,2,1,0:T(8,128)(2,1)S(1)}, bf16[4,6,16,384]{3,2,1,0:T(8,128)(2,1)}, u32[]{:S(2)}) copy-start(bf16[4,6,16,384]{3,2,1,0:T(8,128)(2,1)} %get-tuple-element.14) | copy-start | bytes 884740
  91.3 5.2 %copy-start.7 = (bf16[4,6,16,384]{3,2,1,0:T(8,128)(2,1)S(1)}, bf16[4,6,16,384]{3,2,1,0:T(8,128)(2,1)}, u32[]{:S(2)}) copy-start(bf16[4,6,16,384]{3,2,1,0:T(8,128)(2,1)} %get-tuple-element.29) | copy-start | bytes 884740
  96.1 3.1 %copy-start.11 = (bf16[4,6,16,384]{3,2,1,0:T(8,128)(2,1)S(1)}, bf16[4,6,16,384]{3,2,1,0:T(8,128)(2,1)}, u32[]{:S(2)}) copy-start(bf16[4,6,16,384]{3,2,1,0:T(8,128)(2,1)} %get-tuple-element.25) | copy-start | bytes 884740
  96.8 3.1 %copy-start.10 = (bf16[4,6,16,384]{3,2,1,0:T(8,128)(2,1)S(1)}, bf16[4,6,16,384]{3,2,1,0:T(8,128)(2,1)}, u32[]{:S(2)}) copy-start(bf16[4,6,16,384]{3,2,1,0:T(8,128)(2,1)} %get-tuple-element.26) | copy-start | bytes 884740
  97.2 3.1 %copy-start.9 = (bf16[4,6,16,384]{3,2,1,0:T(8,128)(2,1)S(1)}, bf16[4,6,16,384]{3,2,1,0:T(8,128)(2,1)}, u32[]{:S(2)}) copy-start(bf16[4,6,16,384]{3,2,1,0:T(8,128)(2,1)} %get-tuple-element.27) | copy-start | bytes 884740
  97.5 3.1 %copy-start.8 = (bf16[4,6,16,384]{3,2,1,0:T(8,128)(2,1)S(1)}, bf16[4,6,16,384]{3,2,1,0:T(8,128)(2,1)}, u32[]{:S(2)}) copy-start(bf16[4,6,16,384]{3,2,1,0:T(8,128)(2,1)} %get-tuple-element.24) | copy-start | bytes 884740
  97.9 3.1 %copy-start.6 = (bf16[4,6,16,384]{3,2,1,0:T(8,128)(2,1)S(1)}, bf16[4,6,16,384]{3,2,1,0:T(8,128)(2,1)}, u32[]{:S(2)}) copy-start(bf16[4,6,16,384]{3,2,1,0:T(8,128)(2,1)} %get-tuple-element.5) | copy-start | bytes 884740
  97.9 3.1 %copy-start.24 = (f32[384]{0:T(512)S(1)}, f32[384]{0:T(512)}, u32[]{:S(2)}) copy-start(f32[384]{0:T(512)} %param.13) | copy-start | bytes 4612
Sparse Core Ops, SparseCore 0:
  9.5 75.3 all-gather.1
where the time goes:
time: 110 us; the launch traced here: 109 us
  waiting for transfers between devices  32.7 us (30%)
  matrix products  27 us (25%)
  local copies, waits for them, and re-layouts  19.7 us (18%)
  between operations  14.4 us (13%)
  starting transfers between devices  9.76 us (9%)
  other arithmetic  5.58 us (5%)
    dot_general x54, matrix products, causal_conv(): jnp.dot(window, weight[tap], preferred_element_type=jnp.float32)  27 us
    all_gather x1, waiting for transfers between devices, shards(): kernel_all = lax.all_gather(residual_kernel, 'tm', axis=1, tiled=True)  26.1 us
    reshape x27, local copies, waits for them, and re-layouts, causal_conv(): window = window.reshape(frames_out * LATENT_ROWS * LATENT_COLUMNS, inputs)  12 us
    all_to_all x1, starting transfers between devices, shards(): lax.all_to_all(sharded_latents, 'tm', split_axis=0, concat_axis=1, tiled=...  7.39 us
    slice x32, local copies, waits for them, and re-layouts, causal_conv(): padded[time_tap:time_tap + frames_out, row_tap:row_tap + LATENT_ROWS, col...  5.87 us
    all_to_all x1, waiting for transfers between devices, shards(): lax.all_to_all(sharded_latents, 'tm', split_axis=0, concat_axis=1, tiled=...  5.18 us
    ppermute x1, starting transfers between devices, from_behind(): return lax.ppermute(block, axis, route)  2.37 us
  transfers between devices with their start and end apart: 3, of which 3 were waited for; matrix products, arithmetic and copies ran while one was open for 32% of the time, Pallas kernels for 0%

commit v1 on v0

--- a/solution.py
+++ b/solution.py
@@ -9,6 +9,27 @@
 BLOCK_FRAMES = 4
 LATENT_ROWS = 6
 LATENT_COLUMNS = 16
+
+
+def gather_around(value, axis, dim):
+    count, index, rows = (lax.axis_size(axis), lax.axis_index(axis), value.shape[dim])
+    right = [(i, (i + 1) % count) for i in range(count)]
+    left = [(i, (i - 1) % count) for i in range(count)]
+    out = jnp.zeros((*value.shape[:dim], count * rows, *value.shape[dim + 1 :]), value.dtype)
+    out = lax.dynamic_update_slice_in_dim(out, value, index * rows, axis=dim)
+    from_left = from_right = value
+    middle = count // 2
+    for step in range(1, middle + 1):
+        from_left = lax.ppermute(from_left, axis, right)
+        out = lax.dynamic_update_slice_in_dim(
+            out, from_left, (index - step) % count * rows, axis=dim
+        )
+        if step < count - middle:
+            from_right = lax.ppermute(from_right, axis, left)
+            out = lax.dynamic_update_slice_in_dim(
+                out, from_right, (index + step) % count * rows, axis=dim
+            )
+    return out
 
 
 def from_behind(block, axis, distance):
@@ -78,7 +99,7 @@
     behind = jnp.where(keep, active_all[:2], jnp.zeros_like(active_all[:2]))
     extended = jnp.concatenate([behind, active_all[2:]], axis=0)
     stream = widened[2 * LATENT_ROWS * LATENT_COLUMNS :]
-    kernel_all = lax.all_gather(residual_kernel, "tm", axis=1, tiled=True)
+    kernel_all = gather_around(residual_kernel, "tm", 1)
     branch = causal_conv(extended, kernel_all)
     total = (stream.astype(jnp.float32) + (branch + residual_bias)).reshape(
         BLOCK_FRAMES, LATENT_ROWS, LATENT_COLUMNS, C

time: 110 us -> 202 us (1.84)
  the two profiles are of different devices: /device:TPU:0 before, /device:TPU:22 now
where the time goes in v1:
time: 202 us; the launch traced here: 200 us
  waiting for transfers between devices  66.3 us (33%)
  local copies, waits for them, and re-layouts  62.7 us (31%)
  matrix products  45 us (22%)
  starting transfers between devices  20.5 us (10%)
  other arithmetic  4.12 us (2%)
    ppermute x8, waiting for transfers between devices, gather_around(): from_left = lax.ppermute(from_left, axis, right)  52.8 us
    dot_general x54, matrix products, causal_conv(): jnp.dot(window, weight[tap], preferred_element_type=jnp.float32)  45 us
    reshape x27, local copies, waits for them, and re-layouts, causal_conv(): window = window.reshape(frames_out * LATENT_ROWS * LATENT_COLUMNS, inputs)  20.8 us
    slice x32, local copies, waits for them, and re-layouts, causal_conv(): padded[time_tap:time_tap + frames_out, row_tap:row_tap + LATENT_ROWS, col...  19.8 us
    ppermute x7, starting transfers between devices, gather_around(): from_right = lax.ppermute(from_right, axis, left)  12.8 us
    ppermute x7, waiting for transfers between devices, gather_around(): from_right = lax.ppermute(from_right, axis, left)  8.75 us
    dynamic_update_slice x8, local copies, waits for them, and re-layouts, gather_around(): lax.dynamic_update_slice_in_dim(out, from_left, (index - step) % count *...  7.98 us
    dynamic_update_slice x7, local copies, waits for them, and re-layouts, gather_around(): lax.dynamic_update_slice_in_dim(out, from_right, (index + step) % count *...  7.15 us
  transfers between devices with their start and end apart: 17, of which 12 were waited for; matrix products, arithmetic and copies ran while one was open for 37% of the time, Pallas kernels for 0%

profile of v1, /device:TPU:22, one launch (start us, length us, event | category | flops | bytes accessed | tf_op | source)
XLA Modules:
  0.0 199.8 jit_solution(17754596582333642749)
XLA Ops:
  0.0 1.7 collective-permute-start.2
  2.3 1.4 reduce.2
  4.3 6.3 %all-to-all-start = ((bf16[16,2,192]{2,1,0:T(2,128)(2,1)}), bf16[16,2,192]{2,1,0:T(2,128)(2,1)S(1)}, u32[]{:S(2)}, u32[]{:S(2)}) async-start(bf16[16,2,192]{2,1,0:T(2,128)(2,1)} %reshape.257), calls=%async_computation | async-start | bytes 32768 | tf_op jit(solution)/shard_map/all_to_all | solution.py:82
  10.6 4.3 %broadcast_in_dim.33 = bf16[27,384,384]{2,1,0:T(8,128)(2,1)} broadcast(bf16[]{:T(256)} %constant.124.clone.1), dimensions={} | broadcast | bytes 7962626 | tf_op jit(solution)/shard_map/broadcast_in_dim | solution.py:18
  19.2 4.8 %collective-permute-done = bf16[4,16,96]{2,1,0:T(8,128)(2,1)S(1)} collective-permute-done((bf16[4,16,96]{2,1,0:T(8,128)(2,1)S(1)}, bf16[4,16,96]{2,1,0:T(8,128)(2,1)S(1)}, u32[]{:S(2)}, u32[]{:S(2)}) %collective-permute-start) | collective-permute-done | bytes 12320 | tf_op jit(solution)/shard_map/ppermute | solution.py:38
  24.2 1.4 pad_slice_fusion.28
  28.6 1.7 reshape.202
  30.3 1.6 copy.63
  32.0 1.7 reshape.201
  33.7 1.6 copy.65
  35.3 1.7 reshape.203
  37.0 1.6 copy.66
  38.6 1.7 reshape.204
  40.3 1.6 copy.67
  42.0 1.7 reshape.205
  43.7 1.6 copy.68
  45.3 1.7 reshape.206
  47.0 1.6 copy.69
  48.7 1.7 reshape.207
  50.3 1.6 copy.70
  52.0 1.7 reshape.208
  54.4 1.7 reshape.209
  72.8 1.8 collective-permute-start.4
  74.6 11.4 %collective-permute-done.3 = bf16[27,24,384]{2,1,0:T(8,128)(2,1)S(1)} collective-permute-done((bf16[27,24,384]{2,1,0:T(8,128)(2,1)}, bf16[27,24,384]{2,1,0:T(8,128)(2,1)S(1)}, u32[]{:S(2)}, u32[]{:S(2)}) %collective-permute-start.3) | collective-permute-done | bytes 497696 | tf_op jit(solution)/shard_map/ppermute | solution.py:23
  86.8 3.5 %collective-permute-done.4 = bf16[27,24,384]{2,1,0:T(8,128)(2,1)S(1)} collective-permute-done((bf16[27,24,384]{2,1,0:T(8,128)(2,1)}, bf16[27,24,384]{2,1,0:T(8,128)(2,1)S(1)}, u32[]{:S(2)}, u32[]{:S(2)}) %collective-permute-start.4) | collective-permute-done | bytes 497696 | tf_op jit(solution)/shard_map/ppermute | solution.py:28
  90.4 1.8 collective-permute-start.6
  92.2 7.5 %collective-permute-done.5 = bf16[27,24,384]{2,1,0:T(8,128)(2,1)S(1)} collective-permute-done((bf16[27,24,384]{2,1,0:T(8,128)(2,1)S(1)}, bf16[27,24,384]{2,1,0:T(8,128)(2,1)S(1)}, u32[]{:S(2)}, u32[]{:S(2)}) %collective-permute-start.5) | collective-permute-done | bytes 497696 | tf_op jit(solution)/shard_map/ppermute | solution.py:23
  100.0 3.6 %collective-permute-done.6 = bf16[27,24,384]{2,1,0:T(8,128)(2,1)S(1)} collective-permute-done((bf16[27,24,384]{2,1,0:T(8,128)(2,1)S(1)}, bf16[27,24,384]{2,1,0:T(8,128)(2,1)S(1)}, u32[]{:S(2)}, u32[]{:S(2)}) %collective-permute-start.6) | collective-permute-done | bytes 497696 | tf_op jit(solution)/shard_map/ppermute | solution.py:28
  103.6 1.9 collective-permute-start.8
  105.6 7.4 %collective-permute-done.7 = bf16[27,24,384]{2,1,0:T(8,128)(2,1)S(1)} collective-permute-done((bf16[27,24,384]{2,1,0:T(8,128)(2,1)S(1)}, bf16[27,24,384]{2,1,0:T(8,128)(2,1)S(1)}, u32[]{:S(2)}, u32[]{:S(2)}) %collective-permute-start.7) | collective-permute-done | bytes 497696 | tf_op jit(solution)/shard_map/ppermute | solution.py:23
  113.0 1.4 pad_slice_fusion.23
  114.4 1.9 constant_dynamic-update-slice_fusion.14
  117.2 1.9 collective-permute-start.10
  119.2 1.9 constant_dynamic-update-slice_fusion.13
  121.0 5.6 %collective-permute-done.9 = bf16[27,24,384]{2,1,0:T(8,128)(2,1)S(1)} collective-permute-done((bf16[27,24,384]{2,1,0:T(8,128)(2,1)S(1)}, bf16[27,24,384]{2,1,0:T(8,128)(2,1)S(1)}, u32[]{:S(2)}, u32[]{:S(2)}) %collective-permute-start.9) | collective-permute-done | bytes 497696 | tf_op jit(solution)/shard_map/ppermute | solution.py:23
  130.0 1.9 collective-permute-start.12
  132.7 7.6 %collective-permute-done.11 = bf16[27,24,384]{2,1,0:T(8,128)(2,1)S(1)} collective-permute-done((bf16[27,24,384]{2,1,0:T(8,128)(2,1)S(1)}, bf16[27,24,384]{2,1,0:T(8,128)(2,1)S(1)}, u32[]{:S(2)}, u32[]{:S(2)}) %collective-permute-start.11) | collective-permute-done | bytes 497696 | tf_op jit(solution)/shard_map/ppermute | solution.py:23
  143.0 1.7 collective-permute-start.14
  145.6 8.4 %collective-permute-done.13 = bf16[27,24,384]{2,1,0:T(8,128)(2,1)S(1)} collective-permute-done((bf16[27,24,384]{2,1,0:T(8,128)(2,1)S(1)}, bf16[27,24,384]{2,1,0:T(8,128)(2,1)S(1)}, u32[]{:S(2)}, u32[]{:S(2)}) %collective-permute-start.13) | collective-permute-done | bytes 497696 | tf_op jit(solution)/shard_map/ppermute | solution.py:23
  157.5 4.8 %collective-permute-done.15 = bf16[27,24,384]{2,1,0:T(8,128)(2,1)S(1)} collective-permute-done((bf16[27,24,384]{2,1,0:T(8,128)(2,1)S(1)}, bf16[27,24,384]{2,1,0:T(8,128)(2,1)S(1)}, u32[]{:S(2)}, u32[]{:S(2)}) %collective-permute-start.15) | collective-permute-done | bytes 497696 | tf_op jit(solution)/shard_map/ppermute | solution.py:23
  164.5 1.3 fusion.64
  165.8 1.3 fusion.63
  167.1 1.3 fusion.62
  168.4 1.3 fusion.61
  169.7 1.3 fusion.60
  172.3 1.3 fusion.58
  173.6 1.3 fusion.57
  176.2 1.3 fusion.55
  177.5 1.3 fusion.54
  178.8 1.3 fusion.53
  180.1 1.3 fusion.52
  181.4 1.3 fusion.51
  182.7 1.3 fusion.50
  184.0 1.3 fusion.49
  185.3 1.3 fusion.48
  186.6 1.3 fusion.47
  187.9 1.3 fusion.46
  189.2 1.3 fusion.45
  190.5 1.3 fusion.44
  191.8 1.3 fusion.42
  193.1 1.3 fusion.41
  194.4 1.3 fusion.40
  195.7 1.3 fusion.39
  197.0 1.9 fusion.28
  (155 shorter events, 44.2 us)
Async XLA Ops:
  0.0 14.9 %copy-start = (bf16[27,24,384]{2,1,0:T(8,128)(2,1)S(1)}, bf16[27,24,384]{2,1,0:T(8,128)(2,1)}, u32[]{:S(2)}) copy-start(bf16[27,24,384]{2,1,0:T(8,128)(2,1)} %param.12) | copy-start | bytes 1492996
  0.0 15.8 %copy-start.17 = (s32[8]{0:T(128)S(1)}, s32[8]{0:T(128)}, u32[]{:S(2)}) copy-start(s32[8]{0:T(128)} %param.8) | copy-start | bytes 100
  0.0 72.1 %collective-permute-start.1 = (bf16[27,24,384]{2,1,0:T(8,128)(2,1)}, bf16[27,24,384]{2,1,0:T(8,128)(2,1)}, u32[]{:S(2)}, u32[]{:S(2)}) collective-permute-start(bf16[27,24,384]{2,1,0:T(8,128)(2,1)} %param.12), channel_id=1, source_target_pairs={{0,1},{1,2},{2,3},{3,4},{4,5},{5,6},{6,7},{7,8},{8,9},{9,10},{10,1... | collective-permute-start | bytes 1493000 | tf_op jit(solution)/shard_map/ppermute | solution.py:23
  0.0 72.8 %collective-permute-start.2 = (bf16[27,24,384]{2,1,0:T(8,128)(2,1)}, bf16[27,24,384]{2,1,0:T(8,128)(2,1)}, u32[]{:S(2)}, u32[]{:S(2)}) collective-permute-start(bf16[27,24,384]{2,1,0:T(8,128)(2,1)} %param.12), channel_id=1, source_target_pairs={{0,15},{1,0},{2,1},{3,2},{4,3},{5,4},{6,5},{7,6},{8,7},{9,8},{10,9... | collective-permute-start | bytes 1493000 | tf_op jit(solution)/shard_map/ppermute | solution.py:28
  4.3 12.9 %all-to-all-start = ((bf16[16,2,192]{2,1,0:T(2,128)(2,1)}), bf16[16,2,192]{2,1,0:T(2,128)(2,1)S(1)}, u32[]{:S(2)}, u32[]{:S(2)}) async-start(bf16[16,2,192]{2,1,0:T(2,128)(2,1)} %reshape.257), calls=%async_computation | async-start | bytes 32768 | tf_op jit(solution)/shard_map/all_to_all | solution.py:82
  17.4 6.5 %collective-permute-start = (bf16[4,16,96]{2,1,0:T(8,128)(2,1)S(1)}, bf16[4,16,96]{2,1,0:T(8,128)(2,1)S(1)}, u32[]{:S(2)}, u32[]{:S(2)}) collective-permute-start(bf16[4,16,96]{2,1,0:T(8,128)(2,1)S(1)} %reshape.200), channel_id=1, source_target_pairs={{0,8},{1,9},{2,10},{3,11},{4,12},{5,13},{6,14},{7,15},{16,24},{17,... | collective-permute-start | bytes 36872 | tf_op jit(solution)/shard_map/ppermute | solution.py:38
  56.9 6.8 %copy-start.2 = (bf16[576,16]{0,1:T(8,128)(2,1)S(1)}, bf16[576,16]{0,1:T(8,128)(2,1)}, u32[]{:S(2)}) copy-start(bf16[576,16]{0,1:T(8,128)(2,1)} %reshape.202) | copy-start | bytes 55300
  56.9 7.2 %copy-start.3 = (bf16[576,16]{0,1:T(8,128)(2,1)S(1)}, bf16[576,16]{0,1:T(8,128)(2,1)}, u32[]{:S(2)}) copy-start(bf16[576,16]{0,1:T(8,128)(2,1)} %reshape.203) | copy-start | bytes 55300
  58.7 6.8 %copy-start.4 = (bf16[576,16]{0,1:T(8,128)(2,1)S(1)}, bf16[576,16]{0,1:T(8,128)(2,1)}, u32[]{:S(2)}) copy-start(bf16[576,16]{0,1:T(8,128)(2,1)} %reshape.205) | copy-start | bytes 55300
  59.5 3.9 %copy-start.1 = (bf16[27,16,384]{2,1,0:T(8,128)(2,1)S(1)}, bf16[27,16,384]{2,1,0:T(8,128)(2,1)}, u32[]{:S(2)}) copy-start(bf16[27,16,384]{2,1,0:T(8,128)(2,1)} %param.9) | copy-start | bytes 995332
  60.5 2.9 %copy-start.13 = (bf16[576,16]{0,1:T(8,128)(2,1)S(1)}, bf16[576,16]{0,1:T(8,128)(2,1)}, u32[]{:S(2)}) copy-start(bf16[576,16]{0,1:T(8,128)(2,1)} %reshape.201) | copy-start | bytes 55300
  60.5 5.3 %copy-start.5 = (bf16[576,16]{0,1:T(8,128)(2,1)S(1)}, bf16[576,16]{0,1:T(8,128)(2,1)}, u32[]{:S(2)}) copy-start(bf16[576,16]{0,1:T(8,128)(2,1)} %reshape.206) | copy-start | bytes 55300
  61.2 4.9 %copy-start.6 = (bf16[576,16]{0,1:T(8,128)(2,1)S(1)}, bf16[576,16]{0,1:T(8,128)(2,1)}, u32[]{:S(2)}) copy-start(bf16[576,16]{0,1:T(8,128)(2,1)} %reshape.207) | copy-start | bytes 55300
  61.8 4.6 %copy-start.7 = (bf16[576,16]{0,1:T(8,128)(2,1)S(1)}, bf16[576,16]{0,1:T(8,128)(2,1)}, u32[]{:S(2)}) copy-start(bf16[576,16]{0,1:T(8,128)(2,1)} %reshape.208) | copy-start | bytes 55300
  62.5 4.3 %copy-start.8 = (bf16[576,16]{0,1:T(8,128)(2,1)S(1)}, bf16[576,16]{0,1:T(8,128)(2,1)}, u32[]{:S(2)}) copy-start(bf16[576,16]{0,1:T(8,128)(2,1)} %reshape.209) | copy-start | bytes 55300
  63.2 3.9 %copy-start.9 = (bf16[576,16]{0,1:T(8,128)(2,1)S(1)}, bf16[576,16]{0,1:T(8,128)(2,1)}, u32[]{:S(2)}) copy-start(bf16[576,16]{0,1:T(8,128)(2,1)} %reshape.210) | copy-start | bytes 55300
  63.7 3.7 %copy-start.10 = (bf16[576,16]{0,1:T(8,128)(2,1)S(1)}, bf16[576,16]{0,1:T(8,128)(2,1)}, u32[]{:S(2)}) copy-start(bf16[576,16]{0,1:T(8,128)(2,1)} %reshape.211) | copy-start | bytes 55300
  64.1 3.7 %copy-start.11 = (bf16[576,16]{0,1:T(8,128)(2,1)S(1)}, bf16[576,16]{0,1:T(8,128)(2,1)}, u32[]{:S(2)}) copy-start(bf16[576,16]{0,1:T(8,128)(2,1)} %reshape.212) | copy-start | bytes 55300
  64.4 3.7 %copy-start.12 = (bf16[576,16]{0,1:T(8,128)(2,1)S(1)}, bf16[576,16]{0,1:T(8,128)(2,1)}, u32[]{:S(2)}) copy-start(bf16[576,16]{0,1:T(8,128)(2,1)} %reshape.213) | copy-start | bytes 55300
  69.7 16.4 %copy-start.14 = (f32[384]{0:T(512)S(1)}, f32[384]{0:T(512)}, u32[]{:S(2)}) copy-start(f32[384]{0:T(512)} %param.10) | copy-start | bytes 4612
  70.0 16.5 %copy-start.15 = (f32[384]{0:T(512)S(1)}, f32[384]{0:T(512)}, u32[]{:S(2)}) copy-start(f32[384]{0:T(512)} %param.11) | copy-start | bytes 4612
  72.1 13.9 %collective-permute-start.3 = (bf16[27,24,384]{2,1,0:T(8,128)(2,1)}, bf16[27,24,384]{2,1,0:T(8,128)(2,1)S(1)}, u32[]{:S(2)}, u32[]{:S(2)}) collective-permute-start(bf16[27,24,384]{2,1,0:T(8,128)(2,1)} %collective-permute-done.1), channel_id=1, source_target_pairs={{0,1},{1,2},{2,3},{3,4},{4,5},{5,6},{6,7},{7,8},{8,9},{9,10},{10,1... | collective-permute-start | bytes 1493000 | tf_op jit(solution)/shard_map/ppermute | solution.py:23
  72.8 17.5 %collective-permute-start.4 = (bf16[27,24,384]{2,1,0:T(8,128)(2,1)}, bf16[27,24,384]{2,1,0:T(8,128)(2,1)S(1)}, u32[]{:S(2)}, u32[]{:S(2)}) collective-permute-start(bf16[27,24,384]{2,1,0:T(8,128)(2,1)} %collective-permute-done.2), channel_id=1, source_target_pairs={{0,15},{1,0},{2,1},{3,2},{4,3},{5,4},{6,5},{7,6},{8,7},{9,8},{10,9... | collective-permute-start | bytes 1493000 | tf_op jit(solution)/shard_map/ppermute | solution.py:28
  86.0 13.7 %collective-permute-start.5 = (bf16[27,24,384]{2,1,0:T(8,128)(2,1)S(1)}, bf16[27,24,384]{2,1,0:T(8,128)(2,1)S(1)}, u32[]{:S(2)}, u32[]{:S(2)}) collective-permute-start(bf16[27,24,384]{2,1,0:T(8,128)(2,1)S(1)} %collective-permute-done.3), channel_id=1, source_target_pairs={{0,1},{1,2},{2,3},{3,4},{4,5},{5,6},{6,7},{7,8},{8,9},{9,10},{10,1... | collective-permute-start | bytes 1493000 | tf_op jit(solution)/shard_map/ppermute | solution.py:23
  90.4 13.2 %collective-permute-start.6 = (bf16[27,24,384]{2,1,0:T(8,128)(2,1)S(1)}, bf16[27,24,384]{2,1,0:T(8,128)(2,1)S(1)}, u32[]{:S(2)}, u32[]{:S(2)}) collective-permute-start(bf16[27,24,384]{2,1,0:T(8,128)(2,1)S(1)} %collective-permute-done.4), channel_id=1, source_target_pairs={{0,15},{1,0},{2,1},{3,2},{4,3},{5,4},{6,5},{7,6},{8,7},{9,8},{10,9... | collective-permute-start | bytes 1493000 | tf_op jit(solution)/shard_map/ppermute | solution.py:28
  99.7 13.3 %collective-permute-start.7 = (bf16[27,24,384]{2,1,0:T(8,128)(2,1)S(1)}, bf16[27,24,384]{2,1,0:T(8,128)(2,1)S(1)}, u32[]{:S(2)}, u32[]{:S(2)}) collective-permute-start(bf16[27,24,384]{2,1,0:T(8,128)(2,1)S(1)} %collective-permute-done.5), channel_id=1, source_target_pairs={{0,1},{1,2},{2,3},{3,4},{4,5},{5,6},{6,7},{7,8},{8,9},{9,10},{10,1... | collective-permute-start | bytes 1493000 | tf_op jit(solution)/shard_map/ppermute | solution.py:23
  103.6 13.7 %collective-permute-start.8 = (bf16[27,24,384]{2,1,0:T(8,128)(2,1)S(1)}, bf16[27,24,384]{2,1,0:T(8,128)(2,1)S(1)}, u32[]{:S(2)}, u32[]{:S(2)}) collective-permute-start(bf16[27,24,384]{2,1,0:T(8,128)(2,1)S(1)} %collective-permute-done.6), channel_id=1, source_target_pairs={{0,15},{1,0},{2,1},{3,2},{4,3},{5,4},{6,5},{7,6},{8,7},{9,8},{10,9... | collective-permute-start | bytes 1493000 | tf_op jit(solution)/shard_map/ppermute | solution.py:28
  113.0 13.7 %collective-permute-start.9 = (bf16[27,24,384]{2,1,0:T(8,128)(2,1)S(1)}, bf16[27,24,384]{2,1,0:T(8,128)(2,1)S(1)}, u32[]{:S(2)}, u32[]{:S(2)}) collective-permute-start(bf16[27,24,384]{2,1,0:T(8,128)(2,1)S(1)} %collective-permute-done.7), channel_id=1, source_target_pairs={{0,1},{1,2},{2,3},{3,4},{4,5},{5,6},{6,7},{7,8},{8,9},{9,10},{10,1... | collective-permute-start | bytes 1493000 | tf_op jit(solution)/shard_map/ppermute | solution.py:23
  117.2 12.7 %collective-permute-start.10 = (bf16[27,24,384]{2,1,0:T(8,128)(2,1)S(1)}, bf16[27,24,384]{2,1,0:T(8,128)(2,1)S(1)}, u32[]{:S(2)}, u32[]{:S(2)}) collective-permute-start(bf16[27,24,384]{2,1,0:T(8,128)(2,1)S(1)} %collective-permute-done.8), channel_id=1, source_target_pairs={{0,15},{1,0},{2,1},{3,2},{4,3},{5,4},{6,5},{7,6},{8,7},{9,8},{10,9... | collective-permute-start | bytes 1493000 | tf_op jit(solution)/shard_map/ppermute | solution.py:28
  126.7 13.7 %collective-permute-start.11 = (bf16[27,24,384]{2,1,0:T(8,128)(2,1)S(1)}, bf16[27,24,384]{2,1,0:T(8,128)(2,1)S(1)}, u32[]{:S(2)}, u32[]{:S(2)}) collective-permute-start(bf16[27,24,384]{2,1,0:T(8,128)(2,1)S(1)} %collective-permute-done.9), channel_id=1, source_target_pairs={{0,1},{1,2},{2,3},{3,4},{4,5},{5,6},{6,7},{7,8},{8,9},{9,10},{10,1... | collective-permute-start | bytes 1493000 | tf_op jit(solution)/shard_map/ppermute | solution.py:23
  130.0 13.0 %collective-permute-start.12 = (bf16[27,24,384]{2,1,0:T(8,128)(2,1)S(1)}, bf16[27,24,384]{2,1,0:T(8,128)(2,1)S(1)}, u32[]{:S(2)}, u32[]{:S(2)}) collective-permute-start(bf16[27,24,384]{2,1,0:T(8,128)(2,1)S(1)} %collective-permute-done.10), channel_id=1, source_target_pairs={{0,15},{1,0},{2,1},{3,2},{4,3},{5,4},{6,5},{7,6},{8,7},{9,8},{10,9... | collective-permute-start | bytes 1493000 | tf_op jit(solution)/shard_map/ppermute | solution.py:28
  140.3 13.7 %collective-permute-start.13 = (bf16[27,24,384]{2,1,0:T(8,128)(2,1)S(1)}, bf16[27,24,384]{2,1,0:T(8,128)(2,1)S(1)}, u32[]{:S(2)}, u32[]{:S(2)}) collective-permute-start(bf16[27,24,384]{2,1,0:T(8,128)(2,1)S(1)} %collective-permute-done.11), channel_id=1, source_target_pairs={{0,1},{1,2},{2,3},{3,4},{4,5},{5,6},{6,7},{7,8},{8,9},{9,10},{10,1... | collective-permute-start | bytes 1493000 | tf_op jit(solution)/shard_map/ppermute | solution.py:23
  143.0 13.6 %collective-permute-start.14 = (bf16[27,24,384]{2,1,0:T(8,128)(2,1)S(1)}, bf16[27,24,384]{2,1,0:T(8,128)(2,1)S(1)}, u32[]{:S(2)}, u32[]{:S(2)}) collective-permute-start(bf16[27,24,384]{2,1,0:T(8,128)(2,1)S(1)} %collective-permute-done.12), channel_id=1, source_target_pairs={{0,15},{1,0},{2,1},{3,2},{4,3},{5,4},{6,5},{7,6},{8,7},{9,8},{10,9... | collective-permute-start | bytes 1493000 | tf_op jit(solution)/shard_map/ppermute | solution.py:28
  154.0 8.3 %collective-permute-start.15 = (bf16[27,24,384]{2,1,0:T(8,128)(2,1)S(1)}, bf16[27,24,384]{2,1,0:T(8,128)(2,1)S(1)}, u32[]{:S(2)}, u32[]{:S(2)}) collective-permute-start(bf16[27,24,384]{2,1,0:T(8,128)(2,1)S(1)} %collective-permute-done.13), channel_id=1, source_target_pairs={{0,1},{1,2},{2,3},{3,4},{4,5},{5,6},{6,7},{7,8},{8,9},{9,10},{10,1... | collective-permute-start | bytes 1493000 | tf_op jit(solution)/shard_map/ppermute | solution.py:23
  180.1 17.0 %copy-start.16 = (f32[384]{0:T(512)S(1)}, f32[384]{0:T(512)}, u32[]{:S(2)}) copy-start(f32[384]{0:T(512)} %param.13) | copy-start | bytes 4612
